TPU v7x, 128 devices: a whole 4x4x4 slice. The times are simulated.
128 devices in a mesh: batch: 4 (over y), tp: 4 (over z), ep: 8 (over x, core).
Axes of the slice: x: 4, y: 4, z: 4, core: 2. Of those that a mesh axis runs over, the one named last changes fastest.
Arguments:
- states: bfloat16 [32, 512, 2048], P(('batch', 'ep')), may hold values from -30 to 30
- input_gain: float32 [2048], replicated, may hold values from 0.1 to 1.9
- query_weight: bfloat16 [2048, 4096], P(None, 'tp'), may hold values from -0.125 to 0.125
- key_weight: bfloat16 [2048, 512], P(None, 'tp'), may hold values from -0.125 to 0.125
- value_weight: bfloat16 [2048, 512], P(None, 'tp'), may hold values from -0.125 to 0.125
- query_gain: float32 [128], replicated, may hold values from 1 to 2.5
- key_gain: float32 [128], replicated, may hold values from 0.4 to 1.6
- output_weight: bfloat16 [4096, 2048], P('tp'), may hold values from -0.09375 to 0.09375
- mixture_gain: float32 [2048], replicated, may hold values from 0.1 to 1.9
- expert_gate: bfloat16 [128, 2048, 768], P(('batch', 'tp', 'ep')), may hold values from -0.125 to 0.125
- expert_up: bfloat16 [128, 2048, 768], P(('batch', 'tp', 'ep')), may hold values from -0.125 to 0.125
- expert_down: bfloat16 [128, 768, 2048], P(('batch', 'tp', 'ep')), may hold values from -0.21875 to 0.21875
- gate_scale: float32 [128, 768], P(('batch', 'tp', 'ep')), may hold values from 0.5 to 2
- up_scale: float32 [128, 768], P(('batch', 'tp', 'ep')), may hold values from 0.5 to 2
- down_scale: float32 [128, 2048], P(('batch', 'tp', 'ep')), may hold values from 0.5 to 2
- expert_index: int32 [32, 512, 8], P(('batch', 'ep'), 'tp'), may hold values from 0 to 127, as said below
- expert_slot: int32 [32, 512, 8], P(('batch', 'ep'), 'tp'), may hold values from 0 to 9, as said below
- route_weight: float32 [32, 512, 8], P(('batch', 'ep'), 'tp'), may hold values from 0.05 to 0.35
Outputs:
- layer_output: bfloat16 [32, 512, 2048], P(('batch', 'ep'), 'tp')
Inputs may be any that keep to these rules, and one draw needn't show every extreme that they name: `expert_index`: the 8 experts of a token differ. A pair's positions fall into aligned blocks of 128; within one block no expert is named by more than 10 tokens, in every block some expert is named by exactly 10 tokens, and one expert is named by exactly 10 tokens in every block. `expert_slot`: within one aligned block of 128 positions of a pair, the tokens that name the same expert carry different slots.
All inputs are finite; a program needn't handle non-finite values.
Results may differ from a plain program's by a relative error of at most 0.012.
Values may be sent and summed in bfloat16 or wider, within the bound.
A program may use at most 128 MiB of HBM per device.

v0:
```python
import math

import jax
import jax.numpy as jnp
import numpy as np
from jax import lax
from jax.experimental import pallas as pl
from jax.experimental.pallas import tpu as pltpu
from jax.sharding import PartitionSpec as P

MESH = pl.DeviceIdType.MESH
SETS = (
    ((0, 512), (768, 384), (1408, 384)),
    ((512, 256), (1152, 256), (1792, 256)),
)
CUTS = tuple(cut for cuts in SETS for cut in cuts)
AXES = (("z", "x", "y"), ("x", "y", "z"), ("y", "z", "x"))
FORTH = tuple(range(len(SETS)))
BACK = FORTH[::-1]
BLOCK = 128
CAP = 10
UNIT = 8 * CAP
GROUP = 4 * UNIT
EPS = 1e-06
SEQ = 512
HEAD = 128


def position():
    ep = lax.axis_index("ep")
    return {
        "y": lax.axis_index("batch"),
        "z": lax.axis_index("tp"),
        "x": ep // 2,
        "c": ep % 2,
    }


def moved(me, axis, value):
    there = dict(me)
    there[axis] = value
    return (there["y"], there["z"], there["x"] * 2 + there["c"])


def step(value, distance):
    return lax.rem(value + distance, 4)


def rows_at(index, size):
    return pl.ds(pl.multiple_of(index * size, size), size)


def landed(ref, sem):
    pltpu.make_async_copy(ref, ref, sem).wait()


def push(src, dst, send_sem, recv_sem, device):
    pltpu.make_async_remote_copy(
        src_ref=src,
        dst_ref=dst,
        send_sem=send_sem,
        recv_sem=recv_sem,
        device_id=device,
        device_id_type=MESH,
    ).start()


def routes(me, group, weighted, table, select):
    _, axis_b, axis_c = AXES[group]

    def body(j, carry):
        there = dict(me)
        there[axis_b] = j // 4
        there[axis_c] = j % 4
        expert = (there["y"] * 4 + there["z"]) * 8 + there["x"] * 2 + there["c"]
        first = expert.astype(jnp.float32) * CAP
        for k in range(8):
            top = (CAP * k) // 8 * 8
            slot = lax.broadcasted_iota(jnp.int32, (16, BLOCK), 0) + (top - CAP * k)
            wanted = jnp.where(
                (slot >= 0) & (slot < CAP), slot.astype(jnp.float32) + first, -1.0
            )
            found = jnp.zeros((16, BLOCK), jnp.float32)
            for q in range(8):
                column = table[group, k, q : q + 1, :]
                value = table[group, k, 8 + q : 9 + q, :] if weighted else 1.0
                found = jnp.where(wanted == column, value, found)
            parts = [found]
            if top:
                parts.insert(0, jnp.zeros((top, BLOCK), jnp.float32))
            if top < UNIT - 16:
                parts.append(jnp.zeros((UNIT - 16 - top, BLOCK), jnp.float32))
            select[rows_at(j, UNIT), k * BLOCK : (k + 1) * BLOCK] = jnp.concatenate(
                parts, axis=0
            ).astype(jnp.bfloat16)
        return carry

    lax.fori_loop(0, 16, body, 0)


def layer_kernel(*refs):
    (
        states_hbm,
        input_gain_hbm,
        query_gain_hbm,
        key_gain_hbm,
        cosine_hbm,
        sine_hbm,
        mixture_gain_hbm,
        query_hbm,
        key_hbm,
        value_hbm,
        output_hbm,
        table_hbm,
        swap_hbm,
        gate_scale_hbm,
        up_scale_hbm,
        down_scale_hbm,
        gate_hbm,
        up_hbm,
        down_hbm,
        out_ref,
        rows_ref,
        hidden_ref,
        table_ref,
        table,
        swap_ref,
        gate_scale,
        up_scale,
        down_scale,
        mixture_gain,
        halves,
        arrived,
    ) = refs[:31]
    count = len(CUTS)
    G, M, X, N, R, H, T = [refs[31 + count * i : 31 + count * (i + 1)] for i in range(7)]
    (
        load_sem,
        small_sem,
        w_sem,
        half_send,
        half_recv,
        full_send,
        full_recv,
        p_send,
        p_recv,
        pc_send,
        g_send,
        g_recv,
        gc_send,
        b_send,
        b_recv,
        c_send,
        c_recv,
        rc_send,
        rc_recv,
        rb_send,
        rb_recv,
        k_send,
        k_recv,
        t_send,
        t_recv,
    ) = refs[31 + 7 * count :]
    me = position()
    z = me["z"]
    core = me["c"]
    other = (me["y"], me["z"], me["x"] * 2 + (1 - core))
    ahead = moved(me, "z", step(z, 1))
    behind = moved(me, "z", step(z, 3))

    barrier = pltpu.get_barrier_semaphore()
    for axis in "zxy":
        for d in (1, 2, 3):
            pl.semaphore_signal(
                barrier,
                inc=1,
                device_id=moved(me, axis, step(me[axis], d)),
                device_id_type=MESH,
            )
    pl.semaphore_signal(barrier, inc=1, device_id=other, device_id_type=MESH)

    def block_of(a):
        return core * 4 + a

    def attention(
        input_gain,
        query_gain,
        key_gain,
        cosine,
        sine,
        states,
        normed,
        query_w,
        kv_w,
        output_w,
        queries,
        keys,
        values,
        context,
        leaving,
    ):
        width = states.shape[1]
        half = width // 2
        heads = query_w.shape[1] // HEAD
        loads = [
            pltpu.make_async_copy(src, dst, load_sem.at[n])
            for n, (src, dst) in enumerate(
                (
                    (states_hbm, states),
                    (input_gain_hbm, input_gain),
                    (key_hbm, kv_w.at[:, pl.ds(0, HEAD)]),
                    (value_hbm, kv_w.at[:, pl.ds(HEAD, HEAD)]),
                    (key_gain_hbm, key_gain),
                    (cosine_hbm, cosine),
                    (sine_hbm, sine),
                    (query_gain_hbm, query_gain),
                    (query_hbm, query_w),
                    (output_hbm, output_w),
                )
            )
        ]
        small = [
            pltpu.make_async_copy(src, dst, small_sem.at[n])
            for n, (src, dst) in enumerate(
                (
                    (table_hbm, table_ref),
                    (mixture_gain_hbm, mixture_gain),
                    (swap_hbm, swap_ref),
                    (gate_scale_hbm, gate_scale),
                    (up_scale_hbm, up_scale),
                    (down_scale_hbm, down_scale),
                )
            )
        ]
        for load in loads + small:
            load.start()
        loads[0].wait()
        loads[1].wait()

        def norm(i, carry):
            part = states[rows_at(i, 128), :].astype(jnp.float32)
            scale = lax.rsqrt(jnp.mean(part * part, axis=-1, keepdims=True) + EPS)
            normed[rows_at(i, 128), :] = (part * scale * input_gain[...]).astype(jnp.bfloat16)
            return carry

        lax.fori_loop(0, SEQ // 128, norm, 0)
        for load in loads[2:7]:
            load.wait()
        def turn(part, gain, factor):
            scale = lax.rsqrt(jnp.mean(part * part, axis=-1, keepdims=True) + EPS) * factor
            part = part * gain
            return (
                (part * cosine[...] + pltpu.roll(part, HEAD // 2, 1) * sine[...]) * scale
            ).astype(jnp.bfloat16)

        both = jnp.dot(normed[...], kv_w[...], preferred_element_type=jnp.float32)
        keys[...] = turn(both[:, :HEAD], key_gain[...], 1.0)
        values[:, :HEAD] = both[:, HEAD:].astype(jnp.bfloat16)
        values[:, HEAD:] = jnp.ones((SEQ, HEAD), jnp.bfloat16)
        for load in loads[7:9]:
            load.wait()
        factor = math.log2(math.e) / math.sqrt(HEAD)

        def project(n, carry):
            pair = jnp.dot(
                normed[...], query_w[:, rows_at(n, 2 * HEAD)], preferred_element_type=jnp.float32
            )
            for h in range(2):
                head = turn(pair[:, h * HEAD : (h + 1) * HEAD], query_gain[...], factor)
                for i in range(4):
                    queries[i, rows_at(2 * n + h, BLOCK), :] = head[i * BLOCK : (i + 1) * BLOCK]
            return carry

        lax.fori_loop(0, heads // 2, project, 0)
        pl.semaphore_wait(barrier, 10)
        for load in small:
            load.wait()
        for group in range(3):
            axis = AXES[group][0]
            k = block_of(me[axis])
            pltpu.make_async_copy(table_ref, table.at[group, k], p_recv.at[group, k]).start()
            for d in (1, 3, 2):
                push(
                    table_ref,
                    table.at[group, k],
                    p_send.at[group, d],
                    p_recv.at[group, k],
                    moved(me, axis, step(me[axis], d)),
                )
        loads[9].wait()
        def block(index):
            for n in range(heads // 2):
                scores = lax.dot_general(
                    queries[index, n * 2 * BLOCK : (n + 1) * 2 * BLOCK, :],
                    keys[...],
                    (((1,), (1,)), ((), ())),
                    preferred_element_type=jnp.float32,
                )
                mixed = jnp.dot(
                    jnp.exp2(scores).astype(jnp.bfloat16),
                    values[...],
                    preferred_element_type=jnp.float32,
                )
                mixed = (mixed[:, :HEAD] / mixed[:, HEAD:]).astype(jnp.bfloat16)
                for h in range(2):
                    context[:, (2 * n + h) * HEAD : (2 * n + h + 1) * HEAD] = mixed[
                        h * BLOCK : (h + 1) * BLOCK
                    ]

        def part(side):
            return jnp.dot(
                context[...],
                output_w[:, side * half : (side + 1) * half],
                preferred_element_type=jnp.float32,
            )

        block(step(z, 2))
        for side, device in ((0, ahead), (1, behind)):
            leaving[2, side] = part(side).astype(jnp.bfloat16)
            push(
                leaving.at[2, side], halves.at[side], half_send.at[side], half_recv.at[side], device
            )
        for way, (distance, device) in enumerate(((1, ahead), (3, behind))):
            block(step(z, distance))
            for side in (1 - way, way):
                total = part(side)
                if side == way:
                    landed(halves.at[side], half_recv.at[side])
                    total = total + halves[side].astype(jnp.float32)
                leaving[way, side] = total.astype(jnp.bfloat16)
                push(
                    leaving.at[way, side],
                    arrived.at[way, side],
                    full_send.at[way, side],
                    full_recv.at[way, side],
                    device,
                )
        block(z)
        for side in range(2):
            columns = slice(side * half, (side + 1) * half)
            hidden_ref[:, columns] = part(side) + states[rows_at(z, BLOCK), columns].astype(
                jnp.float32
            )
        for d in range(4):
            for group in range(3):
                k = block_of(step(me[AXES[group][0]], d))
                landed(table.at[group, k], p_recv.at[group, k])
                push(
                    table.at[group, k],
                    table.at[group, k],
                    pc_send.at[group, d],
                    p_recv.at[group, k],
                    other,
                )
        for side in range(2):
            columns = slice(side * half, (side + 1) * half)
            for way in range(2):
                landed(arrived.at[way, side], full_recv.at[way, side])
            hidden_ref[:, columns] = hidden_ref[:, columns] + (
                arrived[0, side].astype(jnp.float32) + arrived[1, side].astype(jnp.float32)
            )
        hidden = hidden_ref[...]
        scale = lax.rsqrt(jnp.mean(hidden * hidden, axis=-1, keepdims=True) + EPS)
        rows_ref[...] = (hidden * scale * mixture_gain[...]).astype(jnp.bfloat16)
        for side in range(2):
            landed(halves.at[side], half_send.at[side])
            for way in range(2):
                landed(arrived.at[way, side], full_send.at[way, side])

    bf16 = jnp.bfloat16
    length, width = states_hbm.shape
    span = query_hbm.shape[1]
    inner = gate_hbm.shape[1]
    pl.run_scoped(
        attention,
        pltpu.VMEM((1, width), jnp.float32),
        pltpu.VMEM((1, HEAD), jnp.float32),
        pltpu.VMEM((1, HEAD), jnp.float32),
        pltpu.VMEM((length, HEAD), jnp.float32),
        pltpu.VMEM((length, HEAD), jnp.float32),
        pltpu.VMEM((length, width), bf16),
        pltpu.VMEM((length, width), bf16),
        pltpu.VMEM((width, span), bf16),
        pltpu.VMEM((width, 2 * HEAD), bf16),
        pltpu.VMEM((span, width), bf16),
        pltpu.VMEM((4, span, HEAD), bf16),
        pltpu.VMEM((length, HEAD), bf16),
        pltpu.VMEM((length, 2 * HEAD), bf16),
        pltpu.VMEM((BLOCK, span), bf16),
        pltpu.VMEM((3, 2, BLOCK, width // 2), bf16),
    )

    def chunks_of(part):
        return [(group, 3 * part + group) + CUTS[3 * part + group] for group in range(3)]

    def place_of(group, beta, gamma):
        return (beta, gamma) if group == 1 else (gamma, beta)

    def experts(gate_w, up_w, down_w, *O):
        weights = [
            pltpu.make_async_copy(src, dst, w_sem.at[n])
            for n, (src, dst) in enumerate(
                ((gate_hbm, gate_w), (up_hbm, up_w), (down_hbm, down_w))
            )
        ]

        def gather(part):
            for group, chunk, start, size in chunks_of(part):
                axis = AXES[group][0]
                a = me[axis]
                k = block_of(a)
                mine = rows_ref.at[:, pl.ds(start, size)]
                place = G[chunk].at[rows_at(k, BLOCK)]
                pltpu.make_async_copy(mine, place, g_recv.at[chunk, k]).start()
                for d in (1, 3, 2):
                    push(
                        mine,
                        place,
                        g_send.at[chunk, d],
                        g_recv.at[chunk, k],
                        moved(me, axis, step(a, d)),
                    )

        def across(part):
            for d in (0, 1, 3, 2):
                for group, chunk, start, size in chunks_of(part):
                    k = block_of(step(me[AXES[group][0]], d))
                    place = G[chunk].at[rows_at(k, BLOCK)]
                    landed(place, g_recv.at[chunk, k])
                    push(place, place, gc_send.at[chunk, d], g_recv.at[chunk, k], other)

        def dispatch(*S):
            gather(0)
            for load in weights:
                load.start()
            for group in range(3):
                for a in range(4):
                    k = (1 - core) * 4 + a
                    landed(table.at[group, k], p_recv.at[group, k])
                routes(me, group, False, table, S[group])
            for part in FORTH:
                across(part)
                if part + 1 < len(SETS):
                    gather(part + 1)
                for group, chunk, start, size in chunks_of(part):
                    axis = AXES[group][1]
                    for a in range(4):
                        k = (1 - core) * 4 + a
                        landed(G[chunk].at[rows_at(k, BLOCK)], g_recv.at[chunk, k])

                    def pick(n, carry, group=group, chunk=chunk, axis=axis):
                        mine = me[axis]
                        beta = step(mine, n + 1)
                        O[chunk][beta] = jnp.dot(
                            S[group][rows_at(beta, GROUP), :],
                            G[chunk][...],
                            preferred_element_type=jnp.float32,
                        ).astype(jnp.bfloat16)

                        @pl.when(n < 3)
                        def _():
                            push(
                                O[chunk].at[beta],
                                M[chunk].at[mine],
                                b_send.at[chunk, n],
                                b_recv.at[chunk, mine],
                                moved(me, axis, beta),
                            )

                        @pl.when(n == 3)
                        def _():
                            pltpu.make_async_copy(
                                O[chunk].at[beta], M[chunk].at[mine], b_recv.at[chunk, mine]
                            ).start()

                        return carry

                    lax.fori_loop(0, 4, pick, 0)

        selections = [pltpu.VMEM((4 * GROUP, 8 * BLOCK), bf16) for _ in range(3)]
        pl.run_scoped(dispatch, *selections)

        for part in FORTH:
            for d in (0, 1, 3, 2):
                for group, chunk, start, size in chunks_of(part):
                    _, axis_b, axis_c = AXES[group]
                    beta = step(me[axis_b], d)
                    mine = me[axis_c]
                    landed(M[chunk].at[beta], b_recv.at[chunk, beta])
                    i, j = place_of(group, beta, mine)
                    for e in (1, 3, 2, 0):
                        gamma = step(mine, e)
                        src = M[chunk].at[beta, rows_at(gamma, UNIT)]
                        dst = X[chunk].at[i, rows_at(j, UNIT)]
                        if e:
                            push(
                                src,
                                dst,
                                c_send.at[chunk, d * 4 + e],
                                c_recv.at[chunk, i * 4 + j],
                                moved(me, axis_c, gamma),
                            )
                        else:
                            pltpu.make_async_copy(src, dst, c_recv.at[chunk, i * 4 + j]).start()

        swap = swap_ref[...]

        def apply(gate_sum, up_sum, activated):
            for load in weights:
                load.wait()
            for part in FORTH:
                chunks = chunks_of(part)
                first_chunk, second_chunk, third_chunk = [entry[1] for entry in chunks]
                for group, chunk, start, size in chunks[::-1]:
                    for i in range(4):
                        for j in range(4):
                            landed(
                                X[chunk].at[i, pl.ds(j * UNIT, UNIT)], c_recv.at[chunk, i * 4 + j]
                            )
                for d in range(4):
                    for e in (1, 2, 3):
                        landed(
                            X[third_chunk].at[0, pl.ds(0, UNIT)], c_send.at[third_chunk, d * 4 + e]
                        )

                def regroup(i, carry, chunk=third_chunk):
                    turned = jnp.dot(
                        swap, X[chunk][i], preferred_element_type=jnp.float32
                    ).astype(jnp.bfloat16)
                    for n in range(4):
                        M[chunk][n, rows_at(i, UNIT), :] = turned[n * UNIT : (n + 1) * UNIT]
                    return carry

                lax.fori_loop(0, 4, regroup, 0)

                def project(y, carry, part=part, chunks=chunks):
                    first = X[chunks[0][1]][y]
                    second = jnp.dot(
                        swap, X[chunks[1][1]][y], preferred_element_type=jnp.float32
                    ).astype(jnp.bfloat16)
                    third = M[chunks[2][1]][y]

                    def product(w, before):
                        total = before[y] if part else None
                        for rows, (_, _, start, size) in zip((first, second, third), chunks):
                            term = jnp.dot(
                                rows, w[start : start + size, :], preferred_element_type=jnp.float32
                            )
                            total = term if total is None else total + term
                        return total

                    gate = product(gate_w, gate_sum)
                    up = product(up_w, up_sum)
                    if part + 1 < len(SETS):
                        gate_sum[y] = gate
                        up_sum[y] = up
                    else:
                        gate = gate * gate_scale[...]
                        activated[y] = (
                            gate / (1.0 + jnp.exp(-gate)) * (up * up_scale[...])
                        ).astype(jnp.bfloat16)
                    return carry

                lax.fori_loop(0, 4, project, 0)

            for chunk in range(count):
                for n in range(3):
                    landed(O[chunk].at[0], b_send.at[chunk, n])

            for part in BACK:
                chunks = chunks_of(part)

                def finish(y, entry):
                    _, _, start, size = entry
                    return (
                        jnp.dot(
                            activated[y],
                            down_w[:, start : start + size],
                            preferred_element_type=jnp.float32,
                        )
                        * down_scale[:, start : start + size]
                    ).astype(jnp.bfloat16)

                def lower(n, carry, chunks=chunks):
                    y = step(me["y"], n + 1)
                    chunk = chunks[0][1]
                    O[chunk][y] = finish(y, chunks[0])

                    @pl.when(n < 3)
                    def _():
                        push(
                            O[chunk].at[y],
                            N[chunk].at[me["y"]],
                            rc_send.at[chunk, n],
                            rc_recv.at[chunk, me["y"]],
                            moved(me, "y", y),
                        )

                    @pl.when(n == 3)
                    def _():
                        pltpu.make_async_copy(
                            O[chunk].at[y], N[chunk].at[me["y"]], rc_recv.at[chunk, me["y"]]
                        ).start()

                    next_chunk = chunks[1][1]
                    O[next_chunk][y] = jnp.dot(
                        swap, finish(y, chunks[1]), preferred_element_type=jnp.float32
                    ).astype(jnp.bfloat16)
                    for e in (1, 3, 2, 0):
                        there = step(me["z"], e)
                        src = O[next_chunk].at[y, rows_at(there, UNIT)]
                        dst = N[next_chunk].at[me["z"], rows_at(y, UNIT)]
                        if e:
                            push(
                                src,
                                dst,
                                rc_send.at[next_chunk, n * 4 + e],
                                rc_recv.at[next_chunk, me["z"] * 4 + y],
                                moved(me, "z", there),
                            )
                        else:
                            pltpu.make_async_copy(
                                src, dst, rc_recv.at[next_chunk, me["z"] * 4 + y]
                            ).start()
                    X[chunks[2][1]][y] = finish(y, chunks[2])
                    return carry

                lax.fori_loop(0, 4, lower, 0)

                def restore(n, carry, chunk=chunks[2][1]):
                    mine = me["x"]
                    x = step(mine, n + 1)
                    parts = jnp.concatenate(
                        [X[chunk][y, rows_at(x, UNIT), :] for y in range(4)], axis=0
                    )
                    O[chunk][x] = jnp.dot(
                        swap, parts, preferred_element_type=jnp.float32
                    ).astype(jnp.bfloat16)

                    @pl.when(n < 3)
                    def _():
                        push(
                            O[chunk].at[x],
                            N[chunk].at[mine],
                            rc_send.at[chunk, n],
                            rc_recv.at[chunk, mine],
                            moved(me, "x", x),
                        )

                    @pl.when(n == 3)
                    def _():
                        pltpu.make_async_copy(
                            O[chunk].at[x], N[chunk].at[mine], rc_recv.at[chunk, mine]
                        ).start()

                    return carry

                lax.fori_loop(0, 4, restore, 0)

        pl.run_scoped(
            apply,
            pltpu.VMEM((4, GROUP, inner), jnp.float32),
            pltpu.VMEM((4, GROUP, inner), jnp.float32),
            pltpu.VMEM((4, GROUP, inner), bf16),
        )

        def collect(*S):
            for group in range(3):
                routes(me, group, True, table, S[group])
            for part in BACK:
                for d in (0, 1, 3, 2):
                    for group, chunk, start, size in chunks_of(part):
                        _, axis_b, axis_c = AXES[group]
                        gamma = step(me[axis_c], d)
                        mine = me[axis_b]
                        if group == 1:
                            for n in range(4):
                                landed(
                                    N[chunk].at[gamma, pl.ds(n * UNIT, UNIT)],
                                    rc_recv.at[chunk, gamma * 4 + n],
                                )
                        else:
                            landed(N[chunk].at[gamma], rc_recv.at[chunk, gamma])
                        for e in (1, 3, 2, 0):
                            beta = step(mine, e)
                            src = N[chunk].at[gamma, rows_at(beta, UNIT)]
                            dst = R[chunk].at[rows_at(mine * 4 + gamma, UNIT)]
                            if e:
                                push(
                                    src,
                                    dst,
                                    rb_send.at[chunk, d * 4 + e],
                                    rb_recv.at[chunk, mine * 4 + gamma],
                                    moved(me, axis_b, beta),
                                )
                            else:
                                pltpu.make_async_copy(
                                    src, dst, rb_recv.at[chunk, mine * 4 + gamma]
                                ).start()
            for chunk, (start, size) in enumerate(CUTS):
                for d in (1, 2, 3):
                    landed(rows_ref.at[:, pl.ds(start, size)], g_send.at[chunk, d])
                for d in range(4):
                    landed(G[chunk].at[pl.ds(0, BLOCK)], gc_send.at[chunk, d])

            def total(group, chunk, half):
                return lax.dot_general(
                    S[group][:, rows_at(half, 512)],
                    R[chunk][...],
                    (((0,), (0,)), ((), ())),
                    preferred_element_type=jnp.float32,
                )

            for part in BACK:
                for group, chunk, start, size in chunks_of(part):
                    for j in range(16):
                        landed(R[chunk].at[pl.ds(j * UNIT, UNIT)], rb_recv.at[chunk, j])
                    G[chunk][512:, :] = total(group, chunk, 1 - core).astype(jnp.bfloat16)
                    push(
                        G[chunk].at[pl.ds(512, 512)], H[chunk], k_send.at[chunk], k_recv.at[chunk], other
                    )
                for group, chunk, start, size in chunks_of(part):
                    axis = AXES[group][0]
                    mine = me[axis]
                    own = total(group, chunk, core)
                    landed(H[chunk], k_recv.at[chunk])
                    G[chunk][:512, :] = (own + H[chunk][...].astype(jnp.float32)).astype(
                        jnp.bfloat16
                    )
                    for d in (1, 3, 2):
                        a = step(mine, d)
                        push(
                            G[chunk].at[rows_at(a, BLOCK)],
                            T[chunk].at[d - 1],
                            t_send.at[chunk, d - 1],
                            t_recv.at[chunk, d - 1],
                            moved(me, axis, a),
                        )

        pl.run_scoped(collect, *selections)
        for part in BACK:
            for group, chunk, start, size in chunks_of(part):
                mine = me[AXES[group][0]]
                result = hidden_ref[:, start : start + size] + G[chunk][
                    rows_at(mine, BLOCK), :
                ].astype(jnp.float32)
                for d in range(3):
                    landed(T[chunk].at[d], t_recv.at[chunk, d])
                    result = result + T[chunk][d].astype(jnp.float32)
                out_ref[:, start : start + size] = result.astype(jnp.bfloat16)

        for group in range(3):
            for d in (1, 2, 3):
                landed(table_ref, p_send.at[group, d])
            for d in range(4):
                landed(table_ref, pc_send.at[group, d])
        for part in BACK:
            for group, chunk, start, size in chunks_of(part):
                for n in range(3):
                    if group != 1:
                        landed(O[chunk].at[0], rc_send.at[chunk, n])
                    landed(T[chunk].at[0], t_send.at[chunk, n])
                landed(H[chunk], k_send.at[chunk])
                for d in range(4):
                    for e in (1, 2, 3):
                        unit = R[chunk].at[pl.ds(0, UNIT)]
                        landed(unit, rb_send.at[chunk, d * 4 + e])
                        if group == 1:
                            landed(unit, rc_send.at[chunk, d * 4 + e])
                        if group != 2:
                            landed(unit, c_send.at[chunk, d * 4 + e])

    pl.run_scoped(
        experts,
        pltpu.VMEM((width, inner), bf16),
        pltpu.VMEM((width, inner), bf16),
        pltpu.VMEM((inner, width), bf16),
        *[pltpu.VMEM((4, GROUP, size), bf16) for _, size in CUTS],
    )


def layer(
    states,
    input_gain,
    query_w,
    key_w,
    value_w,
    query_gain,
    key_gain,
    output_w,
    mixture_gain,
    gate_w,
    up_w,
    down_w,
    gate_scale,
    up_scale,
    down_scale,
    table,
):
    length, width = states.shape
    index = np.arange(HEAD // 2, dtype=np.float64)
    angles = np.arange(length, dtype=np.float64)[:, None] * 1e6 ** (-2.0 * index / HEAD)[None, :]
    cosine = np.concatenate([np.cos(angles)] * 2, axis=1).astype(np.float32)
    sine = np.concatenate([-np.sin(angles), np.sin(angles)], axis=1).astype(np.float32)
    line = np.arange(GROUP)
    a, r = line // UNIT, line % UNIT
    source = ((r % 40) // CAP) * UNIT + (r // 40) * 40 + a * CAP + r % CAP
    swap = (source[:, None] == line[None, :]).astype(jnp.bfloat16)
    dma = pltpu.SemaphoreType.DMA
    bf16 = jnp.bfloat16
    count = len(CUTS)
    hbm = pl.BlockSpec(memory_space=pl.ANY)

    def each(shape):
        return [pltpu.VMEM(shape + (size,), bf16) for _, size in CUTS]

    return pl.pallas_call(
        layer_kernel,
        out_shape=jax.ShapeDtypeStruct((BLOCK, width), bf16),
        in_specs=[hbm] * 19,
        out_specs=pl.BlockSpec(memory_space=pltpu.VMEM),
        scratch_shapes=[
            pltpu.VMEM((BLOCK, width), bf16),
            pltpu.VMEM((BLOCK, width), jnp.float32),
            pltpu.VMEM((16, BLOCK), jnp.float32),
            pltpu.VMEM((3, 8, 16, BLOCK), jnp.float32),
            pltpu.VMEM((GROUP, GROUP), bf16),
            pltpu.VMEM(gate_scale.shape, jnp.float32),
            pltpu.VMEM(up_scale.shape, jnp.float32),
            pltpu.VMEM(down_scale.shape, jnp.float32),
            pltpu.VMEM((1, width), jnp.float32),
            pltpu.VMEM((2, BLOCK, width // 2), bf16),
            pltpu.VMEM((2, 2, BLOCK, width // 2), bf16),
            *each((8 * BLOCK,)),
            *each((4, GROUP)),
            *each((4, GROUP)),
            *each((4, GROUP)),
            *each((4 * GROUP,)),
            *each((4 * BLOCK,)),
            *each((3, BLOCK)),
            dma((10,)),
            dma((6,)),
            dma((3,)),
            dma((2,)),
            dma((2,)),
            dma((2, 2)),
            dma((2, 2)),
            dma((3, 4)),
            dma((3, 8)),
            dma((3, 4)),
            dma((count, 4)),
            dma((count, 8)),
            dma((count, 4)),
            dma((count, 4)),
            dma((count, 4)),
            dma((count, 16)),
            dma((count, 16)),
            dma((count, 16)),
            dma((count, 16)),
            dma((count, 16)),
            dma((count, 16)),
            dma((count,)),
            dma((count,)),
            dma((count, 3)),
            dma((count, 3)),
        ],
        compiler_params=pltpu.CompilerParams(
            collective_id=1, has_side_effects=True, vmem_limit_bytes=65000000
        ),
        cost_estimate=pl.CostEstimate(
            flops=31 * 10**9, bytes_accessed=24 * 10**6, transcendentals=4 * 10**6
        ),
        name="layer",
    )(
        states,
        input_gain[None],
        query_gain[None],
        key_gain[None],
        jnp.asarray(cosine),
        jnp.asarray(sine),
        mixture_gain[None],
        query_w,
        key_w,
        value_w,
        output_w,
        table,
        jnp.asarray(swap),
        gate_scale,
        up_scale,
        down_scale,
        gate_w,
        up_w,
        down_w,
    )


def shards(
    states,
    input_gain,
    query_weight,
    key_weight,
    value_weight,
    query_gain,
    key_gain,
    output_weight,
    mixture_gain,
    expert_gate,
    expert_up,
    expert_down,
    gate_scale,
    up_scale,
    down_scale,
    expert_index,
    expert_slot,
    route_weight,
):
    columns = (expert_index[0] * CAP + expert_slot[0]).astype(jnp.float32)
    table = jnp.concatenate([columns.T, route_weight[0].T], axis=0)
    result = layer(
        states[0],
        input_gain,
        query_weight,
        key_weight,
        value_weight,
        query_gain,
        key_gain,
        output_weight,
        mixture_gain,
        expert_gate[0],
        expert_up[0],
        expert_down[0],
        gate_scale,
        up_scale,
        down_scale,
        table,
    )
    return result[None]


def solution(mesh):
    return jax.shard_map(
        shards,
        mesh=mesh,
        in_specs=(
            P(("batch", "ep"), None, None),
            P(),
            P(None, "tp"),
            P(None, "tp"),
            P(None, "tp"),
            P(),
            P(),
            P("tp", None),
            P(),
            P(("batch", "tp", "ep"), None, None),
            P(("batch", "tp", "ep"), None, None),
            P(("batch", "tp", "ep"), None, None),
            P(("batch", "tp", "ep"), None),
            P(("batch", "tp", "ep"), None),
            P(("batch", "tp", "ep"), None),
            P(("batch", "ep"), "tp", None),
            P(("batch", "ep"), "tp", None),
            P(("batch", "ep"), "tp", None),
        ),
        out_specs=P(("batch", "ep"), "tp", None),
        check_vma=False,
    )
```

profile of v0, /device:TPU:1, one launch (start us, length us, event | category | flops | bytes accessed | tf_op | source)
XLA Modules:
  0.0 179.0 jit_solution(9333308596130240803)
XLA Ops:
  0.0 0.7 convert_bitcast_fusion
  0.7 1.3 pad_maximum_fusion.refs_11_
  2.0 175.1 %layer.1 = bf16[128,2048]{1,0:T(8,128)(2,1)} custom-call(bf16[512,2048]{1,0:T(8,128)(2,1)} %bitcast.21, f32[1,2048]{1,0:T(1,128)} %bitcast.22, f32[1,128]{1,0:T(1,128)} %bitcast.24, f32[1,128]{1,0:T(1,128)} %bitcast.25, f32[512,128]{1,0:T(8,128)} %constant.8.clone.refs_4_, f32[512,128]{1,0:T(8,128)} %constant.9.clone.refs_5_, f32[1,2048]{1,0:T(1,128)} %bitcast.23, ...), custom_call_target="tpu_custom_call" | custom-call | flops 31000000512 | bytes 24000000 | tf_op jit(solution)/shard_map/layer/pallas_call | solution.py:817
  177.1 1.9 %copy.23 = bf16[1,128,2048]{2,1,0:T(8,128)(2,1)} copy(bf16[1,128,2048]{2,1,0:T(8,128)(2,1)} %bitcast.16) | data formatting | bytes 1048576
where the time goes:
time: 179 us
  Pallas kernels  175 us (98%)
  other arithmetic  1.99 us (1%)
  local copies, waits for them, and re-layouts  1.88 us (1%)
    pallas_call x1, Pallas kernels, layer(): pl.pallas_call(layer_kernel, out_shape=jax.ShapeDtypeStruct((BLOCK, width...  175 us

commit v1 on v0

--- a/solution.py
+++ b/solution.py
@@ -16,7 +16,7 @@
 CUTS = tuple(cut for cuts in SETS for cut in cuts)
 AXES = (("z", "x", "y"), ("x", "y", "z"), ("y", "z", "x"))
 FORTH = tuple(range(len(SETS)))
-BACK = FORTH[::-1]
+BACK = FORTH
 BLOCK = 128
 CAP = 10
 UNIT = 8 * CAP
@@ -111,7 +111,9 @@
         key_hbm,
         value_hbm,
         output_hbm,
-        table_hbm,
+        expert_hbm,
+        slot_hbm,
+        route_hbm,
         swap_hbm,
         gate_scale_hbm,
         up_scale_hbm,
@@ -122,6 +124,8 @@
         out_ref,
         rows_ref,
         hidden_ref,
+        expert_ref,
+        slot_ref,
         table_ref,
         table,
         swap_ref,
@@ -131,9 +135,9 @@
         mixture_gain,
         halves,
         arrived,
-    ) = refs[:31]
+    ) = refs[:35]
     count = len(CUTS)
-    G, M, X, N, R, H, T = [refs[31 + count * i : 31 + count * (i + 1)] for i in range(7)]
+    G, M, X, N, R, H, T = [refs[35 + count * i : 35 + count * (i + 1)] for i in range(7)]
     (
         load_sem,
         small_sem,
@@ -160,7 +164,7 @@
         k_recv,
         t_send,
         t_recv,
-    ) = refs[31 + 7 * count :]
+    ) = refs[35 + 7 * count :]
     me = position()
     z = me["z"]
     core = me["c"]
@@ -223,7 +227,9 @@
             pltpu.make_async_copy(src, dst, small_sem.at[n])
             for n, (src, dst) in enumerate(
                 (
-                    (table_hbm, table_ref),
+                    (expert_hbm, expert_ref),
+                    (slot_hbm, slot_ref),
+                    (route_hbm, table_ref.at[pl.ds(8, 8)]),
                     (mixture_gain_hbm, mixture_gain),
                     (swap_hbm, swap_ref),
                     (gate_scale_hbm, gate_scale),
@@ -246,35 +252,25 @@
         lax.fori_loop(0, SEQ // 128, norm, 0)
         for load in loads[2:7]:
             load.wait()
-        def turn(part, gain, factor):
+        def turn(part, gain, factor, cosine, sine):
             scale = lax.rsqrt(jnp.mean(part * part, axis=-1, keepdims=True) + EPS) * factor
             part = part * gain
             return (
-                (part * cosine[...] + pltpu.roll(part, HEAD // 2, 1) * sine[...]) * scale
+                (part * cosine + pltpu.roll(part, HEAD // 2, 1) * sine) * scale
             ).astype(jnp.bfloat16)
 
         both = jnp.dot(normed[...], kv_w[...], preferred_element_type=jnp.float32)
-        keys[...] = turn(both[:, :HEAD], key_gain[...], 1.0)
+        keys[...] = turn(both[:, :HEAD], key_gain[...], 1.0, cosine[...], sine[...])
         values[:, :HEAD] = both[:, HEAD:].astype(jnp.bfloat16)
         values[:, HEAD:] = jnp.ones((SEQ, HEAD), jnp.bfloat16)
         for load in loads[7:9]:
             load.wait()
         factor = math.log2(math.e) / math.sqrt(HEAD)
 
-        def project(n, carry):
-            pair = jnp.dot(
-                normed[...], query_w[:, rows_at(n, 2 * HEAD)], preferred_element_type=jnp.float32
-            )
-            for h in range(2):
-                head = turn(pair[:, h * HEAD : (h + 1) * HEAD], query_gain[...], factor)
-                for i in range(4):
-                    queries[i, rows_at(2 * n + h, BLOCK), :] = head[i * BLOCK : (i + 1) * BLOCK]
-            return carry
-
-        lax.fori_loop(0, heads // 2, project, 0)
         pl.semaphore_wait(barrier, 10)
         for load in small:
             load.wait()
+        table_ref[:8, :] = (expert_ref[...] * CAP + slot_ref[...]).astype(jnp.float32)
         for group in range(3):
             axis = AXES[group][0]
             k = block_of(me[axis])
@@ -289,9 +285,30 @@
                 )
         loads[9].wait()
         def block(index):
+            here = rows_at(index, BLOCK)
+            own_cosine = cosine[here, :]
+            own_sine = sine[here, :]
+
+            def project(n, carry):
+                pair = jnp.dot(
+                    normed[here, :],
+                    query_w[:, rows_at(n, 2 * HEAD)],
+                    preferred_element_type=jnp.float32,
+                )
+                for h in range(2):
+                    queries[rows_at(2 * n + h, BLOCK), :] = turn(
+                        pair[:, h * HEAD : (h + 1) * HEAD],
+                        query_gain[...],
+                        factor,
+                        own_cosine,
+                        own_sine,
+                    )
+                return carry
+
+            lax.fori_loop(0, heads // 2, project, 0)
             for n in range(heads // 2):
                 scores = lax.dot_general(
-                    queries[index, n * 2 * BLOCK : (n + 1) * 2 * BLOCK, :],
+                    queries[n * 2 * BLOCK : (n + 1) * 2 * BLOCK, :],
                     keys[...],
                     (((1,), (1,)), ((), ())),
                     preferred_element_type=jnp.float32,
@@ -383,7 +400,7 @@
         pltpu.VMEM((width, span), bf16),
         pltpu.VMEM((width, 2 * HEAD), bf16),
         pltpu.VMEM((span, width), bf16),
-        pltpu.VMEM((4, span, HEAD), bf16),
+        pltpu.VMEM((span, HEAD), bf16),
         pltpu.VMEM((length, HEAD), bf16),
         pltpu.VMEM((length, 2 * HEAD), bf16),
         pltpu.VMEM((BLOCK, span), bf16),
@@ -392,9 +409,6 @@
 
     def chunks_of(part):
         return [(group, 3 * part + group) + CUTS[3 * part + group] for group in range(3)]
-
-    def place_of(group, beta, gamma):
-        return (beta, gamma) if group == 1 else (gamma, beta)
 
     def experts(gate_w, up_w, down_w, *O):
         weights = [
@@ -451,11 +465,15 @@
                     def pick(n, carry, group=group, chunk=chunk, axis=axis):
                         mine = me[axis]
                         beta = step(mine, n + 1)
-                        O[chunk][beta] = jnp.dot(
-                            S[group][rows_at(beta, GROUP), :],
-                            G[chunk][...],
-                            preferred_element_type=jnp.float32,
-                        ).astype(jnp.bfloat16)
+                        O[chunk][beta] = (
+                            jnp.dot(
+                                S[group][rows_at(beta, GROUP), :],
+                                G[chunk][...],
+                                preferred_element_type=jnp.float32,
+                            )
+                            .astype(jnp.bfloat16)
+                            .reshape(O[chunk].shape[1:])
+                        )
 
                         @pl.when(n < 3)
                         def _():
@@ -480,30 +498,37 @@
         selections = [pltpu.VMEM((4 * GROUP, 8 * BLOCK), bf16) for _ in range(3)]
         pl.run_scoped(dispatch, *selections)
 
+        def arrival(group, chunk, gamma):
+            return X[chunk].at[:, gamma] if group == 1 else X[chunk].at[gamma]
+
         for part in FORTH:
-            for d in (0, 1, 3, 2):
-                for group, chunk, start, size in chunks_of(part):
-                    _, axis_b, axis_c = AXES[group]
-                    beta = step(me[axis_b], d)
-                    mine = me[axis_c]
+            for group, chunk, start, size in chunks_of(part):
+                axis = AXES[group][2]
+                mine = me[axis]
+                for beta in range(4):
                     landed(M[chunk].at[beta], b_recv.at[chunk, beta])
-                    i, j = place_of(group, beta, mine)
-                    for e in (1, 3, 2, 0):
-                        gamma = step(mine, e)
-                        src = M[chunk].at[beta, rows_at(gamma, UNIT)]
-                        dst = X[chunk].at[i, rows_at(j, UNIT)]
-                        if e:
-                            push(
-                                src,
-                                dst,
-                                c_send.at[chunk, d * 4 + e],
-                                c_recv.at[chunk, i * 4 + j],
-                                moved(me, axis_c, gamma),
-                            )
-                        else:
-                            pltpu.make_async_copy(src, dst, c_recv.at[chunk, i * 4 + j]).start()
+                for e in (1, 3, 2, 0):
+                    gamma = step(mine, e)
+                    src = M[chunk].at[:, gamma]
+                    dst = arrival(group, chunk, mine)
+                    if e:
+                        push(
+                            src,
+                            dst,
+                            c_send.at[chunk, e],
+                            c_recv.at[chunk, mine],
+                            moved(me, axis, gamma),
+                        )
+                    else:
+                        pltpu.make_async_copy(src, dst, c_recv.at[chunk, mine]).start()
 
         swap = swap_ref[...]
+
+        def flat(units):
+            return units.reshape(-1, units.shape[-1])
+
+        def units_of(rows):
+            return rows.reshape(-1, UNIT, rows.shape[-1])
 
         def apply(gate_sum, up_sum, activated):
             for load in weights:
@@ -512,33 +537,27 @@
                 chunks = chunks_of(part)
                 first_chunk, second_chunk, third_chunk = [entry[1] for entry in chunks]
                 for group, chunk, start, size in chunks[::-1]:
-                    for i in range(4):
-                        for j in range(4):
-                            landed(
-                                X[chunk].at[i, pl.ds(j * UNIT, UNIT)], c_recv.at[chunk, i * 4 + j]
-                            )
-                for d in range(4):
-                    for e in (1, 2, 3):
-                        landed(
-                            X[third_chunk].at[0, pl.ds(0, UNIT)], c_send.at[third_chunk, d * 4 + e]
-                        )
+                    for gamma in range(4):
+                        landed(arrival(group, chunk, gamma), c_recv.at[chunk, gamma])
+                for e in (1, 2, 3):
+                    landed(X[third_chunk].at[0], c_send.at[third_chunk, e])
 
                 def regroup(i, carry, chunk=third_chunk):
                     turned = jnp.dot(
-                        swap, X[chunk][i], preferred_element_type=jnp.float32
+                        swap, flat(X[chunk][i]), preferred_element_type=jnp.float32
                     ).astype(jnp.bfloat16)
                     for n in range(4):
-                        M[chunk][n, rows_at(i, UNIT), :] = turned[n * UNIT : (n + 1) * UNIT]
+                        M[chunk][n, i] = turned[n * UNIT : (n + 1) * UNIT]
                     return carry
 
                 lax.fori_loop(0, 4, regroup, 0)
 
                 def project(y, carry, part=part, chunks=chunks):
-                    first = X[chunks[0][1]][y]
+                    first = flat(X[chunks[0][1]][y])
                     second = jnp.dot(
-                        swap, X[chunks[1][1]][y], preferred_element_type=jnp.float32
+                        swap, flat(X[chunks[1][1]][y]), preferred_element_type=jnp.float32
                     ).astype(jnp.bfloat16)
-                    third = M[chunks[2][1]][y]
+                    third = flat(M[chunks[2][1]][y])
 
                     def product(w, before):
                         total = before[y] if part else None
@@ -561,7 +580,8 @@
                         ).astype(jnp.bfloat16)
                     return carry
 
-                lax.fori_loop(0, 4, project, 0)
+                if part + 1 < len(SETS):
+                    lax.fori_loop(0, 4, project, 0)
 
             for chunk in range(count):
                 for n in range(3):
@@ -581,10 +601,12 @@
                         * down_scale[:, start : start + size]
                     ).astype(jnp.bfloat16)
 
-                def lower(n, carry, chunks=chunks):
+                def lower(n, carry, part=part, chunks=chunks):
                     y = step(me["y"], n + 1)
+                    if part == BACK[0]:
+                        project(y, 0)
                     chunk = chunks[0][1]
-                    O[chunk][y] = finish(y, chunks[0])
+                    O[chunk][y] = units_of(finish(y, chunks[0]))
 
                     @pl.when(n < 3)
                     def _():
@@ -603,13 +625,15 @@
                         ).start()
 
                     next_chunk = chunks[1][1]
-                    O[next_chunk][y] = jnp.dot(
-                        swap, finish(y, chunks[1]), preferred_element_type=jnp.float32
-                    ).astype(jnp.bfloat16)
+                    O[next_chunk][y] = units_of(
+                        jnp.dot(
+                            swap, finish(y, chunks[1]), preferred_element_type=jnp.float32
+                        ).astype(jnp.bfloat16)
+                    )
                     for e in (1, 3, 2, 0):
                         there = step(me["z"], e)
-                        src = O[next_chunk].at[y, rows_at(there, UNIT)]
-                        dst = N[next_chunk].at[me["z"], rows_at(y, UNIT)]
+                        src = O[next_chunk].at[y, there]
+                        dst = N[next_chunk].at[me["z"], y]
                         if e:
                             push(
                                 src,
@@ -622,7 +646,7 @@
                             pltpu.make_async_copy(
                                 src, dst, rc_recv.at[next_chunk, me["z"] * 4 + y]
                             ).start()
-                    X[chunks[2][1]][y] = finish(y, chunks[2])
+                    X[chunks[2][1]][y] = units_of(finish(y, chunks[2]))
                     return carry
 
                 lax.fori_loop(0, 4, lower, 0)
@@ -631,11 +655,13 @@
                     mine = me["x"]
                     x = step(mine, n + 1)
                     parts = jnp.concatenate(
-                        [X[chunk][y, rows_at(x, UNIT), :] for y in range(4)], axis=0
+                        [X[chunk][y, x] for y in range(4)], axis=0
                     )
-                    O[chunk][x] = jnp.dot(
-                        swap, parts, preferred_element_type=jnp.float32
-                    ).astype(jnp.bfloat16)
+                    O[chunk][x] = units_of(
+                        jnp.dot(swap, parts, preferred_element_type=jnp.float32).astype(
+                            jnp.bfloat16
+                        )
+                    )
 
                     @pl.when(n < 3)
                     def _():
@@ -664,39 +690,39 @@
             pltpu.VMEM((4, GROUP, inner), bf16),
         )
 
-        def collect(*S):
+        def collect(select, *W):
             for group in range(3):
-                routes(me, group, True, table, S[group])
+                routes(me, group, True, table, select)
+
+                def turn(k, carry, group=group):
+                    W[group][rows_at(k, BLOCK), :] = select[:, rows_at(k, BLOCK)].T
+                    return carry
+
+                lax.fori_loop(0, 8, turn, 0)
             for part in BACK:
-                for d in (0, 1, 3, 2):
-                    for group, chunk, start, size in chunks_of(part):
-                        _, axis_b, axis_c = AXES[group]
-                        gamma = step(me[axis_c], d)
-                        mine = me[axis_b]
+                for group, chunk, start, size in chunks_of(part):
+                    axis = AXES[group][1]
+                    mine = me[axis]
+                    for gamma in range(4):
                         if group == 1:
                             for n in range(4):
-                                landed(
-                                    N[chunk].at[gamma, pl.ds(n * UNIT, UNIT)],
-                                    rc_recv.at[chunk, gamma * 4 + n],
-                                )
+                                landed(N[chunk].at[gamma, n], rc_recv.at[chunk, gamma * 4 + n])
                         else:
                             landed(N[chunk].at[gamma], rc_recv.at[chunk, gamma])
-                        for e in (1, 3, 2, 0):
-                            beta = step(mine, e)
-                            src = N[chunk].at[gamma, rows_at(beta, UNIT)]
-                            dst = R[chunk].at[rows_at(mine * 4 + gamma, UNIT)]
-                            if e:
-                                push(
-                                    src,
-                                    dst,
-                                    rb_send.at[chunk, d * 4 + e],
-                                    rb_recv.at[chunk, mine * 4 + gamma],
-                                    moved(me, axis_b, beta),
-                                )
-                            else:
-                                pltpu.make_async_copy(
-                                    src, dst, rb_recv.at[chunk, mine * 4 + gamma]
-                                ).start()
+                    for e in (1, 3, 2, 0):
+                        beta = step(mine, e)
+                        src = N[chunk].at[:, beta]
+                        dst = R[chunk].at[mine]
+                        if e:
+                            push(
+                                src,
+                                dst,
+                                rb_send.at[chunk, e],
+                                rb_recv.at[chunk, mine],
+                                moved(me, axis, beta),
+                            )
+                        else:
+                            pltpu.make_async_copy(src, dst, rb_recv.at[chunk, mine]).start()
             for chunk, (start, size) in enumerate(CUTS):
                 for d in (1, 2, 3):
                     landed(rows_ref.at[:, pl.ds(start, size)], g_send.at[chunk, d])
@@ -704,17 +730,16 @@
                     landed(G[chunk].at[pl.ds(0, BLOCK)], gc_send.at[chunk, d])
 
             def total(group, chunk, half):
-                return lax.dot_general(
-                    S[group][:, rows_at(half, 512)],
-                    R[chunk][...],
-                    (((0,), (0,)), ((), ())),
+                return jnp.dot(
+                    W[group][rows_at(half, 512), :],
+                    flat(R[chunk][...]),
                     preferred_element_type=jnp.float32,
                 )
 
             for part in BACK:
                 for group, chunk, start, size in chunks_of(part):
-                    for j in range(16):
-                        landed(R[chunk].at[pl.ds(j * UNIT, UNIT)], rb_recv.at[chunk, j])
+                    for beta in range(4):
+                        landed(R[chunk].at[beta], rb_recv.at[chunk, beta])
                     G[chunk][512:, :] = total(group, chunk, 1 - core).astype(jnp.bfloat16)
                     push(
                         G[chunk].at[pl.ds(512, 512)], H[chunk], k_send.at[chunk], k_recv.at[chunk], other
@@ -737,7 +762,11 @@
                             moved(me, axis, a),
                         )
 
-        pl.run_scoped(collect, *selections)
+        pl.run_scoped(
+            collect,
+            selections[0],
+            *[pltpu.VMEM((8 * BLOCK, 4 * GROUP), bf16) for _ in range(3)],
+        )
         for part in BACK:
             for group, chunk, start, size in chunks_of(part):
                 mine = me[AXES[group][0]]
@@ -761,21 +790,20 @@
                         landed(O[chunk].at[0], rc_send.at[chunk, n])
                     landed(T[chunk].at[0], t_send.at[chunk, n])
                 landed(H[chunk], k_send.at[chunk])
-                for d in range(4):
-                    for e in (1, 2, 3):
-                        unit = R[chunk].at[pl.ds(0, UNIT)]
-                        landed(unit, rb_send.at[chunk, d * 4 + e])
-                        if group == 1:
-                            landed(unit, rc_send.at[chunk, d * 4 + e])
-                        if group != 2:
-                            landed(unit, c_send.at[chunk, d * 4 + e])
+                for e in (1, 2, 3):
+                    landed(R[chunk].at[0], rb_send.at[chunk, e])
+                    if group != 2:
+                        landed(R[chunk].at[0], c_send.at[chunk, e])
+                    if group == 1:
+                        for n in range(4):
+                            landed(R[chunk].at[0, 0], rc_send.at[chunk, n * 4 + e])
 
     pl.run_scoped(
         experts,
         pltpu.VMEM((width, inner), bf16),
         pltpu.VMEM((width, inner), bf16),
         pltpu.VMEM((inner, width), bf16),
-        *[pltpu.VMEM((4, GROUP, size), bf16) for _, size in CUTS],
+        *[pltpu.VMEM((4, 4, UNIT, size), bf16) for _, size in CUTS],
     )
 
 
@@ -795,7 +823,9 @@
     gate_scale,
     up_scale,
     down_scale,
-    table,
+    expert_index,
+    expert_slot,
+    route_weight,
 ):
     length, width = states.shape
     index = np.arange(HEAD // 2, dtype=np.float64)
@@ -817,11 +847,13 @@
     return pl.pallas_call(
         layer_kernel,
         out_shape=jax.ShapeDtypeStruct((BLOCK, width), bf16),
-        in_specs=[hbm] * 19,
+        in_specs=[hbm] * 21,
         out_specs=pl.BlockSpec(memory_space=pltpu.VMEM),
         scratch_shapes=[
             pltpu.VMEM((BLOCK, width), bf16),
             pltpu.VMEM((BLOCK, width), jnp.float32),
+            pltpu.VMEM((8, BLOCK), jnp.int32),
+            pltpu.VMEM((8, BLOCK), jnp.int32),
             pltpu.VMEM((16, BLOCK), jnp.float32),
             pltpu.VMEM((3, 8, 16, BLOCK), jnp.float32),
             pltpu.VMEM((GROUP, GROUP), bf16),
@@ -832,14 +864,14 @@
             pltpu.VMEM((2, BLOCK, width // 2), bf16),
             pltpu.VMEM((2, 2, BLOCK, width // 2), bf16),
             *each((8 * BLOCK,)),
-            *each((4, GROUP)),
-            *each((4, GROUP)),
-            *each((4, GROUP)),
-            *each((4 * GROUP,)),
+            *each((4, 4, UNIT)),
+            *each((4, 4, UNIT)),
+            *each((4, 4, UNIT)),
+            *each((4, 4, UNIT)),
             *each((4 * BLOCK,)),
             *each((3, BLOCK)),
             dma((10,)),
-            dma((6,)),
+            dma((8,)),
             dma((3,)),
             dma((2,)),
             dma((2,)),
@@ -853,12 +885,12 @@
             dma((count, 4)),
             dma((count, 4)),
             dma((count, 4)),
+            dma((count, 4)),
+            dma((count, 4)),
             dma((count, 16)),
             dma((count, 16)),
-            dma((count, 16)),
-            dma((count, 16)),
-            dma((count, 16)),
-            dma((count, 16)),
+            dma((count, 4)),
+            dma((count, 4)),
             dma((count,)),
             dma((count,)),
             dma((count, 3)),
@@ -883,7 +915,9 @@
         key_w,
         value_w,
         output_w,
-        table,
+        expert_index.T,
+        expert_slot.T,
+        route_weight.T,
         jnp.asarray(swap),
         gate_scale,
         up_scale,
@@ -914,8 +948,6 @@
     expert_slot,
     route_weight,
 ):
-    columns = (expert_index[0] * CAP + expert_slot[0]).astype(jnp.float32)
-    table = jnp.concatenate([columns.T, route_weight[0].T], axis=0)
     result = layer(
         states[0],
         input_gain,
@@ -932,7 +964,9 @@
         gate_scale,
         up_scale,
         down_scale,
-        table,
+        expert_index[0],
+        expert_slot[0],
+        route_weight[0],
     )
     return result[None]
 

time: 179 us -> 167 us (0.933)
  Pallas kernels: 175 us -> 164 us
  other arithmetic: 1.99 us -> 0 us
    pallas_call x1, Pallas kernels: 175 us -> 164 us  [layer(): pl.pallas_call(layer_kernel, out_shape=jax.ShapeDtypeStruct((BLOCK, width...]
where the time goes in v1:
time: 167 us; the launch traced here: 166 us
  Pallas kernels  164 us (98%)
  local copies, waits for them, and re-layouts  1.88 us (1%)
    pallas_call x1, Pallas kernels, layer(): pl.pallas_call(layer_kernel, out_shape=jax.ShapeDtypeStruct((BLOCK, width...  164 us

profile of v1, /device:TPU:1, one launch (start us, length us, event | category | flops | bytes accessed | tf_op | source)
XLA Modules:
  0.0 166.3 jit_solution(9960001041738419989)
XLA Ops:
  0.0 164.4 %layer.1 = bf16[128,2048]{1,0:T(8,128)(2,1)} custom-call(bf16[512,2048]{1,0:T(8,128)(2,1)} %bitcast.22, f32[1,2048]{1,0:T(1,128)} %bitcast.23, f32[1,128]{1,0:T(1,128)} %bitcast.28, f32[1,128]{1,0:T(1,128)} %bitcast.29, f32[512,128]{1,0:T(8,128)} %constant.6.clone.refs_4_, f32[512,128]{1,0:T(8,128)} %constant.7.clone.refs_5_, f32[1,2048]{1,0:T(1,128)} %bitcast.24, ...), custom_call_target="tpu_custom_call" | custom-call | flops 31000000512 | bytes 24000000 | tf_op jit(solution)/shard_map/layer/pallas_call | solution.py:847
  164.5 1.9 %copy.23 = bf16[1,128,2048]{2,1,0:T(8,128)(2,1)} copy(bf16[1,128,2048]{2,1,0:T(8,128)(2,1)} %bitcast.18) | data formatting | bytes 1048576

commit v2 on v1

--- a/solution.py
+++ b/solution.py
@@ -10,8 +10,8 @@
 
 MESH = pl.DeviceIdType.MESH
 SETS = (
-    ((0, 512), (768, 384), (1408, 384)),
-    ((512, 256), (1152, 256), (1792, 256)),
+    ((0, 384), (640, 512), (1408, 384)),
+    ((384, 256), (1152, 256), (1792, 256)),
 )
 CUTS = tuple(cut for cuts in SETS for cut in cuts)
 AXES = (("z", "x", "y"), ("x", "y", "z"), ("y", "z", "x"))
@@ -139,6 +139,7 @@
     count = len(CUTS)
     G, M, X, N, R, H, T = [refs[35 + count * i : 35 + count * (i + 1)] for i in range(7)]
     (
+        state_sem,
         load_sem,
         small_sem,
         w_sem,
@@ -210,7 +211,6 @@
             pltpu.make_async_copy(src, dst, load_sem.at[n])
             for n, (src, dst) in enumerate(
                 (
-                    (states_hbm, states),
                     (input_gain_hbm, input_gain),
                     (key_hbm, kv_w.at[:, pl.ds(0, HEAD)]),
                     (value_hbm, kv_w.at[:, pl.ds(HEAD, HEAD)]),
@@ -238,19 +238,30 @@
                 )
             )
         ]
-        for load in loads + small:
+        quarters = [
+            pltpu.make_async_copy(
+                states_hbm.at[pl.ds(n * BLOCK, BLOCK)],
+                states.at[pl.ds(n * BLOCK, BLOCK)],
+                state_sem.at[n],
+            )
+            for n in range(SEQ // BLOCK)
+        ]
+        for load in quarters + loads[:7]:
             load.start()
         loads[0].wait()
-        loads[1].wait()
 
         def norm(i, carry):
+            landed(states.at[rows_at(i, BLOCK)], state_sem.at[i])
             part = states[rows_at(i, 128), :].astype(jnp.float32)
             scale = lax.rsqrt(jnp.mean(part * part, axis=-1, keepdims=True) + EPS)
             normed[rows_at(i, 128), :] = (part * scale * input_gain[...]).astype(jnp.bfloat16)
             return carry
 
+        loads[7].start()
         lax.fori_loop(0, SEQ // 128, norm, 0)
-        for load in loads[2:7]:
+        for load in loads[8:] + small:
+            load.start()
+        for load in loads[1:6]:
             load.wait()
         def turn(part, gain, factor, cosine, sine):
             scale = lax.rsqrt(jnp.mean(part * part, axis=-1, keepdims=True) + EPS) * factor
@@ -263,7 +274,7 @@
         keys[...] = turn(both[:, :HEAD], key_gain[...], 1.0, cosine[...], sine[...])
         values[:, :HEAD] = both[:, HEAD:].astype(jnp.bfloat16)
         values[:, HEAD:] = jnp.ones((SEQ, HEAD), jnp.bfloat16)
-        for load in loads[7:9]:
+        for load in loads[6:8]:
             load.wait()
         factor = math.log2(math.e) / math.sqrt(HEAD)
 
@@ -283,30 +294,33 @@
                     p_recv.at[group, k],
                     moved(me, axis, step(me[axis], d)),
                 )
-        loads[9].wait()
-        def block(index):
-            here = rows_at(index, BLOCK)
-            own_cosine = cosine[here, :]
-            own_sine = sine[here, :]
+        loads[8].wait()
+        def block(*places):
+            here = [rows_at(place, BLOCK) for place in places]
+            tall = len(here) * BLOCK
+
+            def stacked(ref):
+                return jnp.concatenate([ref[rows, :] for rows in here], axis=0)
 
             def project(n, carry):
                 pair = jnp.dot(
-                    normed[here, :],
+                    stacked(normed),
                     query_w[:, rows_at(n, 2 * HEAD)],
                     preferred_element_type=jnp.float32,
                 )
                 for h in range(2):
-                    queries[rows_at(2 * n + h, BLOCK), :] = turn(
+                    queries[rows_at(2 * n + h, tall), :] = turn(
                         pair[:, h * HEAD : (h + 1) * HEAD],
                         query_gain[...],
                         factor,
-                        own_cosine,
-                        own_sine,
+                        stacked(cosine),
+                        stacked(sine),
                     )
                 return carry
 
             lax.fori_loop(0, heads // 2, project, 0)
-            for n in range(heads // 2):
+            joined = 2 * BLOCK // tall
+            for n in range(heads // joined):
                 scores = lax.dot_general(
                     queries[n * 2 * BLOCK : (n + 1) * 2 * BLOCK, :],
                     keys[...],
@@ -319,14 +333,15 @@
                     preferred_element_type=jnp.float32,
                 )
                 mixed = (mixed[:, :HEAD] / mixed[:, HEAD:]).astype(jnp.bfloat16)
-                for h in range(2):
-                    context[:, (2 * n + h) * HEAD : (2 * n + h + 1) * HEAD] = mixed[
-                        h * BLOCK : (h + 1) * BLOCK
+                for h in range(joined):
+                    head = joined * n + h
+                    context[:tall, head * HEAD : (head + 1) * HEAD] = mixed[
+                        h * tall : (h + 1) * tall
                     ]
 
-        def part(side):
+        def part(side, tall=BLOCK):
             return jnp.dot(
-                context[...],
+                context[:tall, :],
                 output_w[:, side * half : (side + 1) * half],
                 preferred_element_type=jnp.float32,
             )
@@ -337,21 +352,26 @@
             push(
                 leaving.at[2, side], halves.at[side], half_send.at[side], half_recv.at[side], device
             )
-        for way, (distance, device) in enumerate(((1, ahead), (3, behind))):
-            block(step(z, distance))
-            for side in (1 - way, way):
-                total = part(side)
-                if side == way:
-                    landed(halves.at[side], half_recv.at[side])
-                    total = total + halves[side].astype(jnp.float32)
-                leaving[way, side] = total.astype(jnp.bfloat16)
-                push(
-                    leaving.at[way, side],
-                    arrived.at[way, side],
-                    full_send.at[way, side],
-                    full_recv.at[way, side],
-                    device,
-                )
+
+        def leave(way, side, total):
+            leaving[way, side] = total.astype(jnp.bfloat16)
+            push(
+                leaving.at[way, side],
+                arrived.at[way, side],
+                full_send.at[way, side],
+                full_recv.at[way, side],
+                (ahead, behind)[way],
+            )
+
+        block(step(z, 1), step(z, 3))
+        last = part(1, 2 * BLOCK)
+        leave(0, 1, last[:BLOCK])
+        first = part(0, 2 * BLOCK)
+        leave(1, 0, first[BLOCK:])
+        landed(halves.at[0], half_recv.at[0])
+        leave(0, 0, first[:BLOCK] + halves[0].astype(jnp.float32))
+        landed(halves.at[1], half_recv.at[1])
+        leave(1, 1, last[BLOCK:] + halves[1].astype(jnp.float32))
         block(z)
         for side in range(2):
             columns = slice(side * half, (side + 1) * half)
@@ -400,10 +420,10 @@
         pltpu.VMEM((width, span), bf16),
         pltpu.VMEM((width, 2 * HEAD), bf16),
         pltpu.VMEM((span, width), bf16),
-        pltpu.VMEM((span, HEAD), bf16),
+        pltpu.VMEM((2 * span, HEAD), bf16),
         pltpu.VMEM((length, HEAD), bf16),
         pltpu.VMEM((length, 2 * HEAD), bf16),
-        pltpu.VMEM((BLOCK, span), bf16),
+        pltpu.VMEM((2 * BLOCK, span), bf16),
         pltpu.VMEM((3, 2, BLOCK, width // 2), bf16),
     )
 
@@ -870,7 +890,8 @@
             *each((4, 4, UNIT)),
             *each((4 * BLOCK,)),
             *each((3, BLOCK)),
-            dma((10,)),
+            dma((SEQ // BLOCK,)),
+            dma((9,)),
             dma((8,)),
             dma((3,)),
             dma((2,)),

time: 167 us -> 160 us (0.958)
  Pallas kernels: 164 us -> 158 us
    pallas_call x1, Pallas kernels: 164 us -> 158 us  [layer(): pl.pallas_call(layer_kernel, out_shape=jax.ShapeDtypeStruct((BLOCK, width...]
where the time goes in v2:
time: 160 us
  Pallas kernels  158 us (99%)
  local copies, waits for them, and re-layouts  1.88 us (1%)
    pallas_call x1, Pallas kernels, layer(): pl.pallas_call(layer_kernel, out_shape=jax.ShapeDtypeStruct((BLOCK, width...  158 us

profile of v2, /device:TPU:1, one launch (start us, length us, event | category | flops | bytes accessed | tf_op | source)
XLA Modules:
  0.0 159.5 jit_solution(14037528998453223302)
XLA Ops:
  0.0 157.6 %layer.1 = bf16[128,2048]{1,0:T(8,128)(2,1)} custom-call(bf16[512,2048]{1,0:T(8,128)(2,1)} %bitcast.22, f32[1,2048]{1,0:T(1,128)} %bitcast.23, f32[1,128]{1,0:T(1,128)} %bitcast.28, f32[1,128]{1,0:T(1,128)} %bitcast.29, f32[512,128]{1,0:T(8,128)} %constant.6.clone.refs_4_, f32[512,128]{1,0:T(8,128)} %constant.7.clone.refs_5_, f32[1,2048]{1,0:T(1,128)} %bitcast.24, ...), custom_call_target="tpu_custom_call" | custom-call | flops 31000000512 | bytes 24000000 | tf_op jit(solution)/shard_map/layer/pallas_call | solution.py:867
  157.6 1.9 %copy.23 = bf16[1,128,2048]{2,1,0:T(8,128)(2,1)} copy(bf16[1,128,2048]{2,1,0:T(8,128)(2,1)} %bitcast.18) | data formatting | bytes 1048576

commit v3 on v2

--- a/solution.py
+++ b/solution.py
@@ -14,6 +14,7 @@
     ((384, 256), (1152, 256), (1792, 256)),
 )
 CUTS = tuple(cut for cuts in SETS for cut in cuts)
+BASES = tuple(sum(size for _, size in CUTS[:n]) for n in range(len(CUTS) + 1))
 AXES = (("z", "x", "y"), ("x", "y", "z"), ("y", "z", "x"))
 FORTH = tuple(range(len(SETS)))
 BACK = FORTH
@@ -434,7 +435,12 @@
         weights = [
             pltpu.make_async_copy(src, dst, w_sem.at[n])
             for n, (src, dst) in enumerate(
-                ((gate_hbm, gate_w), (up_hbm, up_w), (down_hbm, down_w))
+                [(down_hbm, down_w)]
+                + [
+                    (src.at[pl.ds(start, size)], dst.at[pl.ds(BASES[chunk], size)])
+                    for src, dst in ((gate_hbm, gate_w), (up_hbm, up_w))
+                    for chunk, (start, size) in enumerate(CUTS)
+                ]
             )
         ]
 
@@ -579,14 +585,15 @@
                     ).astype(jnp.bfloat16)
                     third = flat(M[chunks[2][1]][y])
 
+                    rows = jnp.concatenate([first, second, third], axis=1)
+
                     def product(w, before):
-                        total = before[y] if part else None
-                        for rows, (_, _, start, size) in zip((first, second, third), chunks):
-                            term = jnp.dot(
-                                rows, w[start : start + size, :], preferred_element_type=jnp.float32
-                            )
-                            total = term if total is None else total + term
-                        return total
+                        term = jnp.dot(
+                            rows,
+                            w[BASES[3 * part] : BASES[3 * part + 3], :],
+                            preferred_element_type=jnp.float32,
+                        )
+                        return before[y] + term if part else term
 
                     gate = product(gate_w, gate_sum)
                     up = product(up_w, up_sum)
@@ -893,7 +900,7 @@
             dma((SEQ // BLOCK,)),
             dma((9,)),
             dma((8,)),
-            dma((3,)),
+            dma((1 + 2 * count,)),
             dma((2,)),
             dma((2,)),
             dma((2, 2)),

time: 160 us -> 159 us (level)
  no operation moved by 1% of the time
where the time goes in v3:
time: 159 us
  Pallas kernels  157 us (99%)
  local copies, waits for them, and re-layouts  1.88 us (1%)
    pallas_call x1, Pallas kernels, layer(): pl.pallas_call(layer_kernel, out_shape=jax.ShapeDtypeStruct((BLOCK, width...  157 us

profile of v3, /device:TPU:1, one launch (start us, length us, event | category | flops | bytes accessed | tf_op | source)
XLA Modules:
  0.0 158.6 jit_solution(4114592144472006904)
XLA Ops:
  0.0 156.7 %layer.1 = bf16[128,2048]{1,0:T(8,128)(2,1)} custom-call(bf16[512,2048]{1,0:T(8,128)(2,1)} %bitcast.22, f32[1,2048]{1,0:T(1,128)} %bitcast.23, f32[1,128]{1,0:T(1,128)} %bitcast.28, f32[1,128]{1,0:T(1,128)} %bitcast.29, f32[512,128]{1,0:T(8,128)} %constant.6.clone.refs_4_, f32[512,128]{1,0:T(8,128)} %constant.7.clone.refs_5_, f32[1,2048]{1,0:T(1,128)} %bitcast.24, ...), custom_call_target="tpu_custom_call" | custom-call | flops 31000000512 | bytes 24000000 | tf_op jit(solution)/shard_map/layer/pallas_call | solution.py:874
  156.7 1.9 %copy.23 = bf16[1,128,2048]{2,1,0:T(8,128)(2,1)} copy(bf16[1,128,2048]{2,1,0:T(8,128)(2,1)} %bitcast.18) | data formatting | bytes 1048576
